TPU v7x, 32 devices: a whole 2x2x4 slice. The times are simulated.
32 devices in a mesh: blk: 8 (over y, x, core), head: 4 (over z).
Axes of the slice: x: 2, y: 2, z: 4, core: 2. Of those that a mesh axis runs over, the one named last changes fastest.
Arguments:
- query_vectors: bfloat16 [1024, 2560], P('blk', 'head'), may hold values from -8 to 8
- key_vectors: bfloat16 [1024, 2560], P('blk', 'head'), may hold values from -8 to 8, as said below
- value_vectors: bfloat16 [1024, 2560], P('blk', 'head'), may hold values from -6 to 6
- tangent_queries: bfloat16 [1024, 2560], P('blk', 'head'), may hold values from -6 to 6
- tangent_keys: bfloat16 [1024, 2560], P('blk', 'head'), may hold values from -6 to 6
- tangent_values: bfloat16 [1024, 2560], P('blk', 'head'), may hold values from -6 to 6
- target_gap: bfloat16 [1024, 2560], P(('blk', 'head')), may hold values from -6 to 6
Outputs:
- primal_out: bfloat16 [1024, 2560], P(('blk', 'head'))
- tangent_out: bfloat16 [1024, 2560], P(('blk', 'head'))
- query_grad: bfloat16 [1024, 2560], P('blk', 'head')
- key_grad: bfloat16 [1024, 2560], P('blk', 'head')
- value_grad: bfloat16 [1024, 2560], P('blk', 'head')
Inputs may be any that keep to these rules, and one draw needn't show every extreme that they name: `key_vectors`: keys are real-valued draws.
All inputs are finite; a program needn't handle non-finite values.
Results may differ from a plain program's by a relative error of at most 0.015.
Values may be sent and summed in bfloat16 or wider, within the bound.
A program may use at most 128 MiB of HBM per device.

v0:
```python
from functools import partial
import math

import jax
import jax.numpy as jnp
from jax import lax
from jax.sharding import PartitionSpec as P

HD = 128


scale_loss = 64.0
floor_value = -1e30


def split_heads(matrix, head_count):
    return matrix.reshape(matrix.shape[0], head_count, matrix.shape[1] // head_count)


def fold_blocks(advance, running, operands, length):
    block_rows = length
    while block_rows > 512 and block_rows % 2 == 0:
        block_rows = block_rows // 2
    block_total = length // block_rows

    def one_block(position, carried):
        slices = tuple(
            (
                lax.dynamic_slice_in_dim(member, position * block_rows, block_rows, 0)
                for member in operands
            )
        )
        return advance(carried, slices)

    return lax.fori_loop(0, block_total, one_block, running)


def forward_update(nearby, running, slices):
    near_queries, near_tangents, inverse = nearby
    far_keys, far_values, far_tan_keys, far_tan_values = slices
    row_peak, denominator, tan_weight, primal_sum, tangent_sum = running
    scores = (
        jnp.einsum("qhd,khd->qhk", near_queries, far_keys, preferred_element_type=jnp.float32)
        * inverse
    )
    tan_scores = (
        jnp.einsum("qhd,khd->qhk", near_tangents, far_keys, preferred_element_type=jnp.float32)
        + jnp.einsum("qhd,khd->qhk", near_queries, far_tan_keys, preferred_element_type=jnp.float32)
    ) * inverse
    new_peak = jnp.maximum(row_peak, jnp.max(scores, axis=2))
    factor = jnp.exp(row_peak - new_peak)
    weights = jnp.exp(scores - new_peak[:, :, None])
    weighted_tan = weights * tan_scores
    denominator = factor * denominator + jnp.sum(weights, axis=2)
    tan_weight = factor * tan_weight + jnp.sum(weighted_tan, axis=2)
    weights_low = weights.astype(jnp.bfloat16)
    tan_low = weighted_tan.astype(jnp.bfloat16)
    primal_sum = factor[:, :, None] * primal_sum + jnp.einsum(
        "qhk,khd->qhd", weights_low, far_values, preferred_element_type=jnp.float32
    )
    tangent_sum = (
        factor[:, :, None] * tangent_sum
        + jnp.einsum("qhk,khd->qhd", tan_low, far_values, preferred_element_type=jnp.float32)
        + jnp.einsum(
            "qhk,khd->qhd", weights_low, far_tan_values, preferred_element_type=jnp.float32
        )
    )
    return (new_peak, denominator, tan_weight, primal_sum, tangent_sum)


def query_update(nearby, running, slices):
    near_queries, near_cotangent, log_total, inner_sums, inverse = nearby
    far_keys, far_values = slices
    scores = (
        jnp.einsum("qhd,khd->qhk", near_queries, far_keys, preferred_element_type=jnp.float32)
        * inverse
    )
    chances = jnp.exp(scores - log_total[:, :, None])
    prob_grad = jnp.einsum(
        "qhd,khd->qhk", near_cotangent, far_values, preferred_element_type=jnp.float32
    )
    score_grad = (chances * (prob_grad - inner_sums[:, :, None])).astype(jnp.bfloat16)
    return running + jnp.einsum(
        "qhk,khd->qhd", score_grad, far_keys, preferred_element_type=jnp.float32
    )


def key_update(nearby, running, slices):
    near_keys, near_values, inverse = nearby
    far_queries, far_cotangent, far_log, far_inner = slices
    key_acc, value_acc = running
    scores = (
        jnp.einsum("qhd,khd->qhk", far_queries, near_keys, preferred_element_type=jnp.float32)
        * inverse
    )
    chances = jnp.exp(scores - far_log[:, :, None])
    value_acc = value_acc + jnp.einsum(
        "qhk,qhd->khd",
        chances.astype(jnp.bfloat16),
        far_cotangent,
        preferred_element_type=jnp.float32,
    )
    prob_grad = jnp.einsum(
        "qhd,khd->qhk", far_cotangent, near_values, preferred_element_type=jnp.float32
    )
    score_grad = (chances * (prob_grad - far_inner[:, :, None])).astype(jnp.bfloat16)
    key_acc = key_acc + jnp.einsum(
        "qhk,qhd->khd", score_grad, far_queries, preferred_element_type=jnp.float32
    )
    return (key_acc, value_acc)


def per_device(
    query_vectors,
    key_vectors,
    value_vectors,
    tangent_queries,
    tangent_keys,
    tangent_values,
    target_gap,
):
    local_rows = query_vectors.shape[0]
    local_feat = query_vectors.shape[1]
    head_count = local_feat // HD
    inverse = 1.0 / math.sqrt(HD)
    near_queries = split_heads(query_vectors, head_count)
    near_tangents = split_heads(tangent_queries, head_count)
    near_keys = split_heads(key_vectors, head_count)
    near_values = split_heads(value_vectors, head_count)
    row_zeros = jnp.zeros((local_rows, head_count), jnp.float32)
    sum_zeros = jnp.zeros((local_rows, head_count, HD), jnp.float32)
    stats_start = (
        jnp.full((local_rows, head_count), floor_value, jnp.float32),
        row_zeros,
        row_zeros,
        sum_zeros,
        sum_zeros,
    )
    extra_start = ()
    shards = (
        lax.all_gather(key_vectors, "blk", axis=0, tiled=True),
        lax.all_gather(value_vectors, "blk", axis=0, tiled=True),
        lax.all_gather(tangent_keys, "blk", axis=0, tiled=True),
        lax.all_gather(tangent_values, "blk", axis=0, tiled=True),
    )
    stats = stats_start
    extras = extra_start
    operands = tuple((split_heads(member, head_count) for member in shards))
    stats = fold_blocks(
        partial(forward_update, (near_queries, near_tangents, inverse)),
        stats,
        operands,
        shards[0].shape[0],
    )
    stats, extras = (stats, extras)
    row_peak, denominator, tan_weight, primal_sum, tangent_sum = stats
    primal = primal_sum / denominator[:, :, None]
    tangent = (
        tangent_sum / denominator[:, :, None] - (tan_weight / denominator)[:, :, None] * primal
    )
    primal_low = primal.astype(jnp.bfloat16)
    tangent_low = tangent.astype(jnp.bfloat16).reshape(local_rows, -1)
    primal_out, tangent_out = (
        lax.all_to_all(
            primal_low.reshape(local_rows, -1), "head", split_axis=0, concat_axis=1, tiled=True
        ),
        lax.all_to_all(tangent_low, "head", split_axis=0, concat_axis=1, tiled=True),
    )
    token_cotangent = (
        scale_loss * (target_gap.astype(jnp.float32) + tangent_out.astype(jnp.float32))
    ).astype(jnp.bfloat16)
    cotangent = lax.all_to_all(token_cotangent, "head", split_axis=1, concat_axis=0, tiled=True)
    near_cotangent = split_heads(cotangent, head_count)
    log_total = row_peak + jnp.log(denominator)
    inner_sums = jnp.sum(
        near_cotangent.astype(jnp.float32) * primal_low.astype(jnp.float32), axis=2
    )
    all_log, all_inner = (
        lax.all_gather(log_total, "blk", axis=0, tiled=True),
        lax.all_gather(inner_sums, "blk", axis=0, tiled=True),
    )
    query_nearby = (near_queries, near_cotangent, log_total, inner_sums, inverse)
    key_nearby = (near_keys, near_values, inverse)
    shards = (
        lax.all_gather(key_vectors, "blk", axis=0, tiled=True),
        lax.all_gather(value_vectors, "blk", axis=0, tiled=True),
        lax.all_gather(query_vectors, "blk", axis=0, tiled=True),
        lax.all_gather(cotangent, "blk", axis=0, tiled=True),
    )
    query_acc = sum_zeros
    key_acc = sum_zeros
    value_acc = sum_zeros
    length = shards[0].shape[0]
    far_keys, far_values, far_queries, far_cotangent = tuple(
        (split_heads(member, head_count) for member in shards)
    )
    query_acc = fold_blocks(
        partial(query_update, query_nearby), query_acc, (far_keys, far_values), length
    )
    key_acc, value_acc = fold_blocks(
        partial(key_update, key_nearby),
        (key_acc, value_acc),
        (far_queries, far_cotangent, all_log, all_inner),
        length,
    )
    query_acc, key_acc, value_acc = (query_acc, key_acc, value_acc)
    query_grad = (query_acc * inverse).astype(jnp.bfloat16).reshape(local_rows, -1)
    key_grad = (key_acc * inverse).astype(jnp.bfloat16).reshape(local_rows, -1)
    value_grad = value_acc.astype(jnp.bfloat16).reshape(local_rows, -1)
    return (primal_out, tangent_out, query_grad, key_grad, value_grad)


def solution(mesh):
    return jax.shard_map(
        per_device,
        mesh=mesh,
        in_specs=(
            P("blk", "head"),
            P("blk", "head"),
            P("blk", "head"),
            P("blk", "head"),
            P("blk", "head"),
            P("blk", "head"),
            P(("blk", "head"), None),
        ),
        out_specs=(
            P(("blk", "head"), None),
            P(("blk", "head"), None),
            P("blk", "head"),
            P("blk", "head"),
            P("blk", "head"),
        ),
        check_vma=False,
    )
```

profile of v0, /device:TPU:0, one launch (start us, length us, event | category | flops | bytes accessed | tf_op | source)
XLA Modules:
  0.0 217.3 jit_solution(3638347053512219667)
XLA Ops:
  7.2 1.8 copy.145
  9.9 1.7 copy.149
  11.7 1.7 copy.148
  14.9 23.1 %all-gather.7.cloned.1.call-done = bf16[1024,640]{0,1:T(8,128)(2,1)} async-done(((bf16[128,640]{0,1:T(8,128)(2,1)}), bf16[1024,640]{0,1:T(8,128)(2,1)}) %all-gather.7.cloned.1.call-update) | async-done | bytes 1310736 | tf_op jit(solution)/shard_map/all_gather | solution.py:141
  37.9 1.8 copy.151
  39.7 24.7 %all-gather.13.cloned.1.call-done = bf16[1024,640]{1,0:T(8,128)(2,1)} async-done(((bf16[128,640]{1,0:T(8,128)(2,1)}), bf16[1024,640]{1,0:T(8,128)(2,1)}) %all-gather.13.cloned.1.call-update) | async-done | bytes 1310736 | tf_op jit(solution)/shard_map/all_gather | solution.py:144
  64.4 2.4 %copy.150 = bf16[1024,640]{0,1:T(8,128)(2,1)} copy(bf16[1024,640]{1,0:T(8,128)(2,1)} %all-gather.13.cloned.1.call-done) | data formatting | bytes 2621440 | tf_op jit(solution)/shard_map/all_gather | solution.py:144
  66.9 24.8 %all-gather.11.cloned.1.call-done = bf16[1024,640]{0,1:T(8,128)(2,1)} async-done(((bf16[128,640]{0,1:T(8,128)(2,1)}), bf16[1024,640]{0,1:T(8,128)(2,1)}) %all-gather.11.cloned.1.call-update) | async-done | bytes 1310736 | tf_op jit(solution)/shard_map/all_gather | solution.py:142
  91.6 27.1 %all-gather.9.cloned.1.call-done = bf16[1024,640]{0,1:T(8,128)(2,1)} async-done(((bf16[128,640]{0,1:T(8,128)(2,1)}), bf16[1024,640]{0,1:T(8,128)(2,1)}) %all-gather.9.cloned.1.call-update) | async-done | bytes 1310736 | tf_op jit(solution)/shard_map/all_gather | solution.py:143
  118.7 9.5 %while.52 = (s32[]{:T(128)}, f32[128,5]{0,1:T(8,128)S(1)}, f32[128,5]{0,1:T(8,128)S(1)}, f32[128,5]{0,1:T(8,128)S(1)}, f32[128,5,128]{0,2,1:T(8,128)S(1)}, /*ind...) while((s32[]{:T(128)}, f32[128,5]{0,1:T(8,128)S(1)}, ...), condition=%wide.region_4.0_spmd.clone, body=%wide.region_0.0_spmd.clone.sunk | while | flops 508481920 | bytes 32673596 | solution.py:35
  129.5 11.6 %all_to_all.57 = bf16[4,32,640]{2,1,0:T(8,128)(2,1)S(1)} all-to-all(bf16[4,32,640]{2,1,0:T(8,128)(2,1)S(1)} %all_to_all.46), channel_id=1, replica_groups=mesh['blk'=8,'head'=4] {'head'}, dimensions={0} | all-to-all | bytes 327680 | tf_op jit(solution)/shard_map/all_to_all | solution.py:167
  141.9 9.8 %all_to_all.58 = bf16[32,4,640]{2,0,1:T(8,128)(2,1)} all-to-all(bf16[32,4,640]{2,0,1:T(8,128)(2,1)S(1)} %bitcast.152), channel_id=1, replica_groups=mesh['blk'=8,'head'=4] {'head'}, dimensions={1} | all-to-all | bytes 327680 | tf_op jit(solution)/shard_map/all_to_all | solution.py:172
  153.9 9.0 %all_gather.31 = f32[1024,5]{0,1:T(8,128)S(1)} all-gather(f32[128,5]{0,1:T(8,128)S(1)} %get-tuple-element.1071), channel_id=1, replica_groups=mesh['blk'=8,'head'=4] {'blk'}, dimensions={0}, use_global_device_ids=true | all-gather | bytes 23040 | tf_op jit(solution)/shard_map/all_gather | solution.py:179
  166.0 4.0 %all-to-all-start = ((bf16[4,32,640]{2,1,0:T(8,128)(2,1)}), bf16[4,32,640]{2,1,0:T(8,128)(2,1)}, u32[]{:S(2)}, u32[]{:S(2)}) async-start(bf16[4,32,640]{2,1,0:T(8,128)(2,1)} %all_to_all.42), calls=%async_computation | async-start | bytes 327680 | tf_op jit(solution)/shard_map/all_to_all | solution.py:164
  170.0 6.9 %while.53 = (s32[]{:T(128)}, f32[128,5,128]{0,2,1:T(8,128)}, bf16[1024,5,128]{2,0,1:T(8,128)(2,1)S(1)}, bf16[128,5,128]{2,0,1:T(8,128)(2,1)S(1)}, f32[128,5]{0,1...) while((s32[]{:T(128)}, f32[128,5,128]{0,2,1:T(8,128)}, ...), condition=%wide.region_7.0_spmd.clone, body=%wide.region_6.0_spmd.clone.sunk | while | flops 253460480 | bytes 5577392 | solution.py:35
  174.5 2.4 %fusion.137 = f32[128,5,128]{0,2,1:T(8,128)} fusion(f32[128,5,512]{0,2,1:T(8,128)S(1)} %fusion.136, bf16[128,5,128]{2,0,1:T(8,128)(2,1)S(1)} %get-tuple-element.1094, f32[128,5]{0,1:T(8,128)S(1)} %get-tuple-element.1095, bf16[1024,5,128]{2,0,1:T(8,128)(2,1)S(1)} %get-tuple-element.1093, s32[]{:T(128)S(6)} %select_n.35, ...), kind=kOutput, calls=%fused_computation.47.clone.1 | convolution fusion | flops 169246720 | bytes 3444736 | tf_op jit(solution)/shard_map/while/body/eval_jaxpr/qhk,khd->qhd/dot_general | solution.py:83
  176.9 9.0 %all_gather.33 = f32[1024,5]{1,0:T(8,128)S(1)} all-gather(f32[128,5]{1,0:T(8,128)S(1)} %get-tuple-element.814), channel_id=1, replica_groups=mesh['blk'=8,'head'=4] {'blk'}, dimensions={0}, use_global_device_ids=true | all-gather | bytes 23040 | tf_op jit(solution)/shard_map/all_gather | solution.py:180
  188.6 1.6 copy.169
  190.2 10.4 %all-gather.15.cloned.1.call-done = bf16[1024,640]{0,1:T(8,128)(2,1)} async-done(((bf16[128,640]{0,1:T(8,128)(2,1)}), bf16[1024,640]{0,1:T(8,128)(2,1)}) %all-gather.15.cloned.1.call-update) | async-done | bytes 1310736 | tf_op jit(solution)/shard_map/all_gather | solution.py:187
  200.7 8.1 %while.54 = (s32[]{:T(128)}, f32[128,5,128]{0,2,1:T(8,128)S(1)}, f32[128,5,128]{0,2,1:T(8,128)S(1)}, bf16[1024,5,128]{0,2,1:T(8,128)(2,1)}, bf16[128,5,128]{2,0,...) while((s32[]{:T(128)}, f32[128,5,128]{0,2,1:T(8,128)S(1)}, ...), condition=%wide.region_9.0_spmd.clone, body=%wide.region_8.0_spmd.clone.sunk | while | flops 337838080 | bytes 8261313 | solution.py:35
  200.7 1.7 fusion.145
  202.7 2.0 fusion.146
  204.7 1.7 fusion.145
  206.8 2.0 fusion.146
  (110 shorter events, 28.4 us)
Async XLA Ops:
  7.2 6.3 %copy-start.9 = (bf16[128,640]{1,0:T(8,128)(2,1)S(1)}, bf16[128,640]{1,0:T(8,128)(2,1)}, u32[]{:S(2)}) copy-start(bf16[128,640]{1,0:T(8,128)(2,1)} %param.13) | copy-start | bytes 491524
  7.2 6.7 %copy-start.10 = (bf16[128,640]{1,0:T(8,128)(2,1)S(1)}, bf16[128,640]{1,0:T(8,128)(2,1)}, u32[]{:S(2)}) copy-start(bf16[128,640]{1,0:T(8,128)(2,1)} %param.16) | copy-start | bytes 491524
  7.2 30.7 %all-gather.7.cloned.1.call-start = ((), (), s32[]{:S(2)}) async-start(), calls=%async_computation.3 | async-start | bytes 1474560 | tf_op jit(solution)/shard_map/all_gather | solution.py:141
  9.1 55.4 %all-gather.13.cloned.1.call-start = ((), (), s32[]{:S(2)}) async-start(), calls=%async_computation.6 | async-start | bytes 1474560 | tf_op jit(solution)/shard_map/all_gather | solution.py:144
  9.8 81.8 %all-gather.11.cloned.1.call-start = ((), (), s32[]{:S(2)}) async-start(), calls=%async_computation.5 | async-start | bytes 1474560 | tf_op jit(solution)/shard_map/all_gather | solution.py:142
  11.6 107.1 %all-gather.9.cloned.1.call-start = ((), (), s32[]{:S(2)}) async-start(), calls=%async_computation.4 | async-start | bytes 1474560 | tf_op jit(solution)/shard_map/all_gather | solution.py:143
  13.4 175.2 %all-gather.17.cloned.1.call-start = ((), (), s32[]{:S(2)}) async-start(), calls=%async_computation.8 | async-start | bytes 1474560 | tf_op jit(solution)/shard_map/all_gather | solution.py:188
  13.7 24.2 %copy-start.5 = (bf16[128,640]{0,1:T(8,128)(2,1)}, bf16[128,640]{0,1:T(8,128)(2,1)S(1)}, u32[]{:S(2)}) copy-start(bf16[128,640]{0,1:T(8,128)(2,1)S(1)} %copy.146) | copy-start | bytes 491524
  119.1 1.4 copy-start.3
  120.5 1.3 copy-start.1
  121.1 1.4 copy-start
  123.8 1.4 copy-start.3
  125.2 1.3 copy-start.1
  125.8 1.4 copy-start
  128.9 12.3 %copy-start.11 = (bf16[32,2560]{1,0:T(8,128)(2,1)S(1)}, bf16[32,2560]{1,0:T(8,128)(2,1)}, u32[]{:S(2)}) copy-start(bf16[32,2560]{1,0:T(8,128)(2,1)} %param.19) | copy-start | bytes 491524
  129.3 23.0 %copy-start.6 = (bf16[128,640]{0,1:T(8,128)(2,1)S(1)}, bf16[128,640]{0,1:T(8,128)(2,1)}, u32[]{:S(2)}) copy-start(bf16[128,640]{0,1:T(8,128)(2,1)} %copy.145) | copy-start | bytes 491524
  129.5 23.6 %copy-start.7 = (bf16[128,640]{0,1:T(8,128)(2,1)S(1)}, bf16[128,640]{0,1:T(8,128)(2,1)}, u32[]{:S(2)}) copy-start(bf16[128,640]{0,1:T(8,128)(2,1)} %copy.149) | copy-start | bytes 491524
  141.2 0.7 copy-start.8
  151.6 49.0 %all-gather.15.cloned.1.call-start = ((), (), s32[]{:S(2)}) async-start(), calls=%async_computation.7 | async-start | bytes 1474560 | tf_op jit(solution)/shard_map/all_gather | solution.py:187
  166.0 21.0 %all-to-all-start = ((bf16[4,32,640]{2,1,0:T(8,128)(2,1)}), bf16[4,32,640]{2,1,0:T(8,128)(2,1)}, u32[]{:S(2)}, u32[]{:S(2)}) async-start(bf16[4,32,640]{2,1,0:T(8,128)(2,1)} %all_to_all.42), calls=%async_computation | async-start | bytes 327680 | tf_op jit(solution)/shard_map/all_to_all | solution.py:164
  176.9 9.2 %copy-start.2 = (f32[128,5,128]{0,2,1:T(8,128)S(1)}, f32[128,5,128]{0,2,1:T(8,128)}, u32[]{:S(2)}) copy-start(f32[128,5,128]{0,2,1:T(8,128)} %get-tuple-element.507) | copy-start | bytes 983044
  188.6 12.1 %copy-start.4 = (bf16[128,5,128]{2,0,1:T(8,128)(2,1)S(1)}, bf16[128,5,128]{2,0,1:T(8,128)(2,1)}, u32[]{:S(2)}) copy-start(bf16[128,5,128]{2,0,1:T(8,128)(2,1)} %copy.172) | copy-start | bytes 491524
Sparse Core Ops, SparseCore 0:
  10.5 27.4 all-gather.6
  39.8 24.5 all-gather.12
  66.9 24.7 all-gather.10
  94.0 24.7 all-gather.8
  151.8 22.3 all-gather.16
  175.9 24.7 all-gather.14
where the time goes:
time: 218 us; the launch traced here: 217 us
  waiting for transfers between devices  111 us (51%)
  blocking collectives  39.4 us (18%)
  local copies, waits for them, and re-layouts  24.7 us (11%)
  matrix products  21.6 us (10%)
  between operations  14.4 us (7%)
  starting transfers between devices  4.22 us (2%)
    all_gather x1, waiting for transfers between devices, per_device(): lax.all_gather(tangent_keys, 'blk', axis=0, tiled=True)  27.1 us
    all_gather x1, waiting for transfers between devices, per_device(): lax.all_gather(value_vectors, 'blk', axis=0, tiled=True)  24.8 us
    all_gather x1, waiting for transfers between devices, per_device(): lax.all_gather(tangent_values, 'blk', axis=0, tiled=True)  24.7 us
    all_gather x1, waiting for transfers between devices, per_device(): lax.all_gather(key_vectors, 'blk', axis=0, tiled=True)  23.1 us
    unnamed x34, local copies, waits for them, and re-layouts  14 us
    all_to_all x1, blocking collectives, per_device(): lax.all_to_all(tangent_low, 'head', split_axis=0, concat_axis=1, tiled=True)  11.6 us
    all_gather x1, waiting for transfers between devices, per_device(): lax.all_gather(query_vectors, 'blk', axis=0, tiled=True)  10.4 us
    all_to_all x1, blocking collectives, per_device(): lax.all_to_all(token_cotangent, 'head', split_axis=1, concat_axis=0, tile...  9.76 us
  transfers between devices with their start and end apart: 7, of which 5 were waited for; matrix products, arithmetic and copies ran while one was open for 11% of the time, Pallas kernels for 0%

commit v1 on v0

v1 whole, which is shorter than its diff:
```python
import functools
import math

import jax
import jax.numpy as jnp
from jax import lax
from jax.experimental import pallas as pl
from jax.experimental.pallas import tpu as pltpu
from jax.sharding import PartitionSpec as P

HD = 128
MESH = pl.DeviceIdType.MESH

scale_loss = 64.0


def owner_of(head, nb):
    return (2 * head) % nb + (2 * head) // nb


def nt_dot(a, b):
    return lax.dot_general(a, b, (((1,), (1,)), ((), ())), preferred_element_type=jnp.float32)


def nn_dot(a, b):
    return jnp.dot(a, b, preferred_element_type=jnp.float32)


def kernel(nb, nh, hc, q_in, k_in, v_in, tq_in, tk_in, tv_in, g_in,
           po, to, dq, dk, dv,
           kk, qq, vv, gg, vt, kt, po_s, to_s, dq_s, dk_s, dv_s, dk_acc, dv_acc,
           in_send, in_recv, out_send, out_recv):
    b = lax.axis_index("blk")
    z = lax.axis_index("head")
    me = b * nh + z
    rows = q_in.shape[0]
    few = g_in.shape[0]
    seq = kk.shape[0]
    mine = b // 2 + (b % 2) * (nb // 2)
    is_owner = mine < hc
    inverse = 1.0 / math.sqrt(HD)
    log2e = 1.0 / math.log(2.0)

    barrier = pltpu.get_barrier_semaphore()

    def greet(p, carry):
        @pl.when(p != me)
        def _():
            pl.semaphore_signal(
                barrier, inc=1, device_id=(p // nh, p % nh), device_id_type=MESH
            )
        return carry

    lax.fori_loop(0, nb * nh, greet, 0)
    pl.semaphore_wait(barrier, nb * nh - 1)

    def send(src, dst, s_sem, r_sem, to_b, to_z):
        away = jnp.logical_or(to_b != b, to_z != z)

        @pl.when(away)
        def _():
            pltpu.make_async_remote_copy(
                src_ref=src, dst_ref=dst, send_sem=s_sem, recv_sem=r_sem,
                device_id=(to_b, to_z), device_id_type=MESH,
            ).start()

        @pl.when(jnp.logical_not(away))
        def _():
            pltpu.make_async_copy(src, dst, r_sem).start()

    def arrived(ref, sem):
        pltpu.make_async_copy(ref, ref, sem).wait()

    my_rows = pl.ds(pl.multiple_of(b * rows, rows), rows)
    inbound = (
        (k_in, kk, 0), (q_in, qq, 1), (tk_in, kk, 1), (tq_in, qq, 0),
        (v_in, vv, 0), (tv_in, vv, 1),
    )
    for at, (src, dst, half) in enumerate(inbound):
        for head in range(hc):
            send(
                src.at[:, pl.ds(head * HD, HD)],
                dst.at[my_rows, pl.ds(half * HD, HD)],
                in_send.at[at], in_recv.at[at], owner_of(head, nb), z,
            )
    few_rows = pl.ds(pl.multiple_of(me * few, few), few)
    for head in range(hc):
        def send_gap(plane, carry, head=head):
            columns = pl.ds(pl.multiple_of((plane * hc + head) * HD, HD), HD)
            send(
                g_in.at[:, columns], gg.at[few_rows, :],
                in_send.at[6], in_recv.at[6], owner_of(head, nb), plane,
            )
            return carry
        lax.fori_loop(0, nh, send_gap, 0)

    @pl.when(is_owner)
    def _():
        for at, (src, dst, half) in enumerate(inbound):
            arrived(dst.at[:, pl.ds(half * HD, HD)], in_recv.at[at])
        arrived(gg, in_recv.at[6])
        vt[...] = vv[...].T
        kt[...] = kk[:, :HD].T
        dk_acc[...] = jnp.zeros_like(dk_acc)
        dv_acc[...] = jnp.zeros_like(dv_acc)
        block = 256
        tiles = block // rows
        own_columns = pl.ds(pl.multiple_of(mine * HD, HD), HD)
        wide_columns = pl.ds(pl.multiple_of((z * hc + mine) * HD, HD), HD)

        def one_block(i, carry):
            at = pl.ds(pl.multiple_of(i * block, block), block)
            pair = qq[at, :]
            query = pair[:, HD:]
            s = nt_dot(kk[:, :HD], query)
            t = nt_dot(kk[...], pair)
            peak = jnp.max(s, axis=0, keepdims=True)
            w = jnp.exp2((s - peak) * (inverse * log2e))
            wt = w * t
            total = jnp.sum(w, axis=0, keepdims=True)
            tan_total = jnp.sum(wt, axis=0, keepdims=True)
            w_low = w.astype(jnp.bfloat16)
            t_low = wt.astype(jnp.bfloat16)
            sums = nn_dot(vt[...], w_low)
            more = nn_dot(vt[:HD, :], t_low)
            r = 1.0 / total
            primal = sums[:HD] * r
            tangent = (more * inverse + sums[HD:]) * r - (tan_total * inverse * r) * primal
            primal_low = primal.astype(jnp.bfloat16)
            tangent_low = tangent.astype(jnp.bfloat16)
            gap = gg[at, :].T.astype(jnp.float32)
            cot = (scale_loss * (gap + tangent_low.astype(jnp.float32))).astype(jnp.bfloat16)
            cot_r = (cot.astype(jnp.float32) * r).astype(jnp.bfloat16)
            inner = jnp.sum(
                cot_r.astype(jnp.float32) * primal_low.astype(jnp.float32), axis=0, keepdims=True
            )
            dp = nn_dot(vv[:, :HD], cot_r)
            ds = (w * (dp - inner)).astype(jnp.bfloat16)
            po_s[at, :] = primal_low.T
            to_s[at, :] = tangent_low.T
            dq_s[at, :] = (nn_dot(kt[...], ds) * inverse).astype(jnp.bfloat16).T
            dk_acc[...] += nn_dot(ds, query)
            dv_acc[...] += nn_dot(w_low, cot_r.T)
            for tile in range(tiles):
                to_b = i * tiles + tile
                start = pl.multiple_of(to_b * rows, rows)
                for plane in range(nh):
                    part = pl.ds(pl.multiple_of(start + plane * few, few), few)
                    send(po_s.at[part, :], po.at[:, wide_columns],
                         out_send.at[0], out_recv.at[0], to_b, plane)
                    send(to_s.at[part, :], to.at[:, wide_columns],
                         out_send.at[1], out_recv.at[1], to_b, plane)
                send(dq_s.at[pl.ds(start, rows), :], dq.at[:, own_columns],
                     out_send.at[2], out_recv.at[2], to_b, z)
            return carry

        lax.fori_loop(0, seq // block, one_block, 0)
        dk_s[...] = (dk_acc[...] * inverse).astype(jnp.bfloat16)
        dv_s[...] = dv_acc[...].astype(jnp.bfloat16)

        def send_grads(to_b, carry):
            part = pl.ds(pl.multiple_of(to_b * rows, rows), rows)
            send(dk_s.at[part, :], dk.at[:, own_columns],
                 out_send.at[3], out_recv.at[3], to_b, z)
            send(dv_s.at[part, :], dv.at[:, own_columns],
                 out_send.at[4], out_recv.at[4], to_b, z)
            return carry

        lax.fori_loop(0, nb, send_grads, 0)

    for at, ref in enumerate((po, to, dq, dk, dv)):
        arrived(ref, out_recv.at[at])

    @pl.when(is_owner)
    def _():
        for at, (src, dst, half) in enumerate(inbound):
            arrived(src.at[:, pl.ds(0, (hc - 1) * HD)], in_send.at[at])
        arrived(g_in.at[:, pl.ds(0, (nh * hc - 1) * HD)], in_send.at[6])
        for at, ref in enumerate((po_s, to_s)):
            arrived(ref.at[pl.ds(0, seq - few), :], out_send.at[at])
        for at, ref in enumerate((dq_s, dk_s, dv_s)):
            arrived(ref.at[pl.ds(0, seq - rows), :], out_send.at[at + 2])

    @pl.when(jnp.logical_not(is_owner))
    def _():
        for at, (src, dst, half) in enumerate(inbound):
            arrived(src, in_send.at[at])
        arrived(g_in, in_send.at[6])


def per_device(nb, nh, q, k, v, tq, tk, tv, g):
    rows, feat = q.shape
    hc = feat // HD
    seq = rows * nb
    low = jnp.bfloat16
    anywhere = pl.BlockSpec(memory_space=pl.ANY)
    wide = jax.ShapeDtypeStruct(g.shape, low)
    narrow = jax.ShapeDtypeStruct(q.shape, low)
    return pl.pallas_call(
        functools.partial(kernel, nb, nh, hc),
        out_shape=(wide, wide, narrow, narrow, narrow),
        in_specs=[anywhere] * 7,
        out_specs=(anywhere,) * 5,
        scratch_shapes=[
            pltpu.VMEM((seq, 2 * HD), low),
            pltpu.VMEM((seq, 2 * HD), low),
            pltpu.VMEM((seq, 2 * HD), low),
            pltpu.VMEM((seq, HD), low),
            pltpu.VMEM((2 * HD, seq), low),
            pltpu.VMEM((HD, seq), low),
            pltpu.VMEM((seq, HD), low),
            pltpu.VMEM((seq, HD), low),
            pltpu.VMEM((seq, HD), low),
            pltpu.VMEM((seq, HD), low),
            pltpu.VMEM((seq, HD), low),
            pltpu.VMEM((seq, HD), jnp.float32),
            pltpu.VMEM((seq, HD), jnp.float32),
            pltpu.SemaphoreType.DMA((7,)),
            pltpu.SemaphoreType.DMA((7,)),
            pltpu.SemaphoreType.DMA((5,)),
            pltpu.SemaphoreType.DMA((5,)),
        ],
        compiler_params=pltpu.CompilerParams(
            collective_id=0, has_side_effects=True, vmem_limit_bytes=58 * 2**20
        ),
    )(q, k, v, tq, tk, tv, g)


def solution(mesh):
    nb, nh = mesh.shape["blk"], mesh.shape["head"]
    narrow = P("blk", "head")
    wide = P(("blk", "head"), None)
    return jax.shard_map(
        functools.partial(per_device, nb, nh),
        mesh=mesh,
        in_specs=(narrow,) * 6 + (wide,),
        out_specs=(wide, wide, narrow, narrow, narrow),
        check_vma=False,
    )
```

time: 218 us -> 58.6 us (0.27)
  waiting for transfers between devices: 111 us -> 0 us
  Pallas kernels: 0 us -> 52.5 us
  blocking collectives: 39.4 us -> 0 us
  matrix products: 21.6 us -> 0 us
  local copies, waits for them, and re-layouts: 24.7 us -> 5.22 us
  between operations: 14.4 us -> 0.66 us
  starting transfers between devices: 4.22 us -> 0 us
    all_gather x6 -> x0, waiting for transfers between devices: 110 us -> none  [the longest x1 27.1 us: per_device(): lax.all_gather(tangent_keys, 'blk', axis=0, tiled=True)]
    pallas_call x0 -> x1, Pallas kernels: none -> 52.5 us  [per_device(): pl.pallas_call(functools.partial(kernel, nb, nh, hc), out_shape=(wide, wi...]
    dot_general x22 -> x0, matrix products: 21.6 us -> none  [the longest x2 3.91 us: key_update(): jnp.einsum('qhk,qhd->khd', score_grad, far_queries, preferred_element_typ...]
    all_to_all x2 -> x0, blocking collectives: 21.4 us -> none  [the longest x1 11.6 us: per_device(): lax.all_to_all(tangent_low, 'head', split_axis=0, concat_axis=1, tiled=True)]
    all_gather x2 -> x0, blocking collectives: 18 us -> none  [the longest x1 9.01 us: per_device(): lax.all_gather(log_total, 'blk', axis=0, tiled=True)]
    unnamed x34 -> x13, local copies, waits for them, and re-layouts: 14 us -> 5.22 us
    all_gather x2 -> x0, local copies, waits for them, and re-layouts: 4.09 us -> none  [the longest x1 2.45 us: per_device(): lax.all_gather(tangent_values, 'blk', axis=0, tiled=True)]
    all_to_all x1 -> x0, starting transfers between devices: 3.97 us -> none  [per_device(): lax.all_to_all(primal_low.reshape(local_rows, -1), 'head', split_axis=0,...]
  transfers between devices with their start and end apart: 7 -> 0, of which waited for: 5 -> 0; matrix products, arithmetic and copies ran while one was open for 11% -> 0% of each run, Pallas kernels for 0% -> 0%
where the time goes in v1:
time: 58.6 us; the launch traced here: 58.4 us
  Pallas kernels  52.5 us (90%)
  local copies, waits for them, and re-layouts  5.22 us (9%)
  between operations  0.66 us (1%)
    pallas_call x1, Pallas kernels, per_device(): pl.pallas_call(functools.partial(kernel, nb, nh, hc), out_shape=(wide, wi...  52.5 us
    unnamed x13, local copies, waits for them, and re-layouts  5.22 us

profile of v1, /device:TPU:0, one launch (start us, length us, event | category | flops | bytes accessed | tf_op | source)
XLA Modules:
  0.0 58.4 jit_solution(15132777631795188008)
XLA Ops:
  0.6 52.5 %shard_map.110 = (bf16[32,2560]{1,0:T(8,128)(2,1)}, bf16[32,2560]{1,0:T(8,128)(2,1)}, bf16[128,640]{1,0:T(8,128)(2,1)}, bf16[128,640]{1,0:T(8,128)(2,1)}, bf16[128,640]{1,0:T(8,128)(2,1)}) custom-call(bf16[128,640]{1,0:T(8,128)(2,1)} %q_in.1, bf16[128,640]{1,0:T(8,128)(2,1)} %k_in.1, bf16[128,640]{1,0:T(8,128)(2,1)} %v_in.1, bf16[128,640]{1,0:T(8,128)(2,1)} %tq_in.1, ...), custom_call_target="tpu_custom_call" | custom-call | tf_op jit(solution)/shard_map/pallas_call | solution.py:199
  53.2 0.0 copy-start.3
  53.2 1.6 %copy.17 = bf16[32,2560]{1,0:T(8,128)(2,1)} copy(bf16[32,2560]{1,0:T(8,128)(2,1)} %get-tuple-element.10) | data formatting | bytes 327680
  54.8 0.0 copy-done.3
  54.8 0.0 copy-start.2
  54.8 0.7 %copy.18 = bf16[32,2560]{1,0:T(8,128)(2,1)} copy(bf16[32,2560]{1,0:T(8,128)(2,1)S(1)} %copy-done.3) | data formatting | bytes 327680
  55.5 0.3 copy-done.2
  55.8 0.0 copy-start.1
  55.8 0.7 %copy.19 = bf16[128,640]{1,0:T(8,128)(2,1)} copy(bf16[128,640]{1,0:T(8,128)(2,1)S(1)} %copy-done.2) | data formatting | bytes 327680
  56.5 0.3 copy-done.1
  56.8 0.0 copy-start
  56.8 0.7 %copy.20 = bf16[128,640]{1,0:T(8,128)(2,1)} copy(bf16[128,640]{1,0:T(8,128)(2,1)S(1)} %copy-done.1) | data formatting | bytes 327680
  57.5 0.3 copy-done
  57.8 0.7 %copy.21 = bf16[128,640]{1,0:T(8,128)(2,1)} copy(bf16[128,640]{1,0:T(8,128)(2,1)S(1)} %copy-done) | data formatting | bytes 327680
Async XLA Ops:
  53.2 1.6 %copy-start.3 = (bf16[32,2560]{1,0:T(8,128)(2,1)S(1)}, bf16[32,2560]{1,0:T(8,128)(2,1)}, u32[]{:S(2)}) copy-start(bf16[32,2560]{1,0:T(8,128)(2,1)} %get-tuple-element.11) | copy-start | bytes 491524
  54.8 1.0 %copy-start.2 = (bf16[128,640]{1,0:T(8,128)(2,1)S(1)}, bf16[128,640]{1,0:T(8,128)(2,1)}, u32[]{:S(2)}) copy-start(bf16[128,640]{1,0:T(8,128)(2,1)} %get-tuple-element.12) | copy-start | bytes 491524
  55.8 1.0 %copy-start.1 = (bf16[128,640]{1,0:T(8,128)(2,1)S(1)}, bf16[128,640]{1,0:T(8,128)(2,1)}, u32[]{:S(2)}) copy-start(bf16[128,640]{1,0:T(8,128)(2,1)} %get-tuple-element.13) | copy-start | bytes 491524
  56.8 1.0 %copy-start = (bf16[128,640]{1,0:T(8,128)(2,1)S(1)}, bf16[128,640]{1,0:T(8,128)(2,1)}, u32[]{:S(2)}) copy-start(bf16[128,640]{1,0:T(8,128)(2,1)} %get-tuple-element.14) | copy-start | bytes 491524

commit v2 on v1

v2 whole, which is shorter than its diff:
```python
import functools
import math

import jax
import jax.numpy as jnp
from jax import lax
from jax.experimental import pallas as pl
from jax.experimental.pallas import tpu as pltpu
from jax.sharding import PartitionSpec as P

HD = 128
MESH = pl.DeviceIdType.MESH

scale_loss = 64.0


def nt_dot(a, b):
    return lax.dot_general(a, b, (((1,), (1,)), ((), ())), preferred_element_type=jnp.float32)


def nn_dot(a, b):
    return jnp.dot(a, b, preferred_element_type=jnp.float32)


def kernel(nb, nh, hc, q_in, k_in, v_in, tq_in, tk_in, tv_in, g_in,
           po, to, dq, dk, dv,
           kk, qq, vv, gg, vt, kt, po_s, to_s, dq_s, dk_s, dv_s, dk_acc, dv_acc,
           g_mid, po_mid, to_mid, dk_part, dv_part, dk_sum, dv_sum,
           in_send, in_recv, out_send, out_recv, mid_send, mid_recv, part_recv, sum_sem):
    b = lax.axis_index("blk")
    z = lax.axis_index("head")
    rows = q_in.shape[0]
    few = g_in.shape[0]
    seq = kk.shape[0]
    group = hc * HD
    block = 2 * rows
    last = hc - 1
    odd = b % 2
    helper = odd == 1
    owner = jnp.logical_and(odd == 0, b // 2 < last)
    idle = jnp.logical_and(odd == 0, b // 2 >= last)
    mine = (b // 2) * (1 - odd) + last * odd
    inverse = 1.0 / math.sqrt(HD)
    log2e = 1.0 / math.log(2.0)

    barrier = pltpu.get_barrier_semaphore()
    for step in range(1, nb):
        pl.semaphore_signal(
            barrier, inc=1, device_id=((b + step) % nb, z), device_id_type=MESH
        )
    for step in range(1, nh):
        pl.semaphore_signal(
            barrier, inc=1, device_id=(b, (z + step) % nh), device_id_type=MESH
        )
    pl.semaphore_wait(barrier, nb + nh - 2)

    def send(src, dst, s_sem, r_sem, to_b, to_z):
        away = jnp.logical_or(to_b != b, to_z != z)

        @pl.when(away)
        def _():
            pltpu.make_async_remote_copy(
                src_ref=src, dst_ref=dst, send_sem=s_sem, recv_sem=r_sem,
                device_id=(to_b, to_z), device_id_type=MESH,
            ).start()

        @pl.when(jnp.logical_not(away))
        def _():
            pltpu.make_async_copy(src, dst, r_sem).start()

    def arrived(ref, sem):
        pltpu.make_async_copy(ref, ref, sem).wait()

    def swap_planes(src_of, dst, at, s_sems, r_sems):
        for plane in range(nh):
            send(src_of(plane), dst, s_sems.at[at], r_sems.at[at], b, plane)

    my_rows = pl.ds(pl.multiple_of(b * rows, rows), rows)
    few_rows = pl.ds(pl.multiple_of(z * few, few), few)
    swap_planes(lambda plane: g_in.at[:, pl.ds(plane * group, group)],
                g_mid.at[few_rows, :], 2, mid_send, mid_recv)

    keys = ((k_in, kk, 0, 0), (tk_in, kk, 1, 2), (v_in, vv, 0, 4), (tv_in, vv, 1, 5))
    queries = ((q_in, qq, 1, 1), (tq_in, qq, 0, 3), (g_mid, gg, 0, 6))
    inbound = (keys[0], queries[0], keys[1], queries[1], keys[2], keys[3], queries[2])
    for member in inbound:
        src, dst, half, at = member
        if src is g_mid:
            arrived(g_mid, mid_recv.at[2])
        tail = src.at[:, pl.ds(last * HD, HD)]
        place = dst.at[my_rows, pl.ds(half * HD, HD)]
        for head in range(last):
            send(src.at[:, pl.ds(head * HD, HD)], place,
                 in_send.at[at], in_recv.at[at], 2 * head, z)
        if at in (0, 2, 4, 5):
            for step in range(nb // 2):
                send(tail, place, in_send.at[at], in_recv.at[at], 2 * step + 1, z)
        else:
            send(tail, place, in_send.at[at], in_recv.at[at], 2 * (b // 2) + 1, z)

    own_columns = pl.ds(pl.multiple_of(mine * HD, HD), HD)

    @pl.when(jnp.logical_not(idle))
    def _():
        for src, dst, half, at in keys:
            arrived(dst.at[:, pl.ds(half * HD, HD)], in_recv.at[at])
        for src, dst, half, at in queries:
            @pl.when(owner)
            def _():
                arrived(dst.at[:, pl.ds(half * HD, HD)], in_recv.at[at])

            @pl.when(helper)
            def _():
                arrived(
                    dst.at[pl.ds(pl.multiple_of((b // 2) * block, block), block),
                           pl.ds(half * HD, HD)],
                    in_recv.at[at],
                )
        vt[...] = vv[...].T
        kt[...] = kk[:, :HD].T
        dk_acc[...] = jnp.zeros_like(dk_acc)
        dv_acc[...] = jnp.zeros_like(dv_acc)

        def one_block(i, carry):
            at = pl.ds(pl.multiple_of(i * block, block), block)
            pair = qq[at, :]
            query = pair[:, HD:]
            s = nt_dot(kk[:, :HD], query)
            t = nt_dot(kk[...], pair)
            peak = jnp.max(s, axis=0, keepdims=True)
            w = jnp.exp2((s - peak) * (inverse * log2e))
            wt = w * t
            total = jnp.sum(w, axis=0, keepdims=True)
            tan_total = jnp.sum(wt, axis=0, keepdims=True)
            w_low = w.astype(jnp.bfloat16)
            t_low = wt.astype(jnp.bfloat16)
            sums = nn_dot(vt[...], w_low)
            more = nn_dot(vt[:HD, :], t_low)
            r = 1.0 / total
            primal = sums[:HD] * r
            tangent = (more * inverse + sums[HD:]) * r - (tan_total * inverse * r) * primal
            primal_low = primal.astype(jnp.bfloat16)
            tangent_low = tangent.astype(jnp.bfloat16)
            gap = gg[at, :].T.astype(jnp.float32)
            cot = (scale_loss * (gap + tangent_low.astype(jnp.float32))).astype(jnp.bfloat16)
            cot_r = (cot.astype(jnp.float32) * r).astype(jnp.bfloat16)
            inner = jnp.sum(
                cot_r.astype(jnp.float32) * primal_low.astype(jnp.float32), axis=0, keepdims=True
            )
            dp = nn_dot(vv[:, :HD], cot_r)
            ds = (w * (dp - inner)).astype(jnp.bfloat16)
            po_s[at, :] = primal_low.T
            to_s[at, :] = tangent_low.T
            dq_s[at, :] = (nn_dot(kt[...], ds) * inverse).astype(jnp.bfloat16).T
            dk_acc[...] += nn_dot(ds, query)
            dv_acc[...] += nn_dot(w_low, cot_r.T)
            for tile in range(2):
                to_b = 2 * i + tile
                part = pl.ds(pl.multiple_of(to_b * rows, rows), rows)
                send(po_s.at[part, :], po_mid.at[:, own_columns],
                     out_send.at[0], mid_recv.at[0], to_b, z)
                send(to_s.at[part, :], to_mid.at[:, own_columns],
                     out_send.at[1], mid_recv.at[1], to_b, z)
                send(dq_s.at[part, :], dq.at[:, own_columns],
                     out_send.at[2], out_recv.at[2], to_b, z)
            return carry

        first = odd * (b // 2)
        count = odd + (1 - odd) * (seq // block)
        lax.fori_loop(first, first + count, one_block, 0)
        dk_s[...] = (dk_acc[...] * inverse).astype(jnp.bfloat16)
        dv_s[...] = dv_acc[...].astype(jnp.bfloat16)

        @pl.when(owner)
        def _():
            for to_b in range(nb):
                part = pl.ds(to_b * rows, rows)
                send(dk_s.at[part, :], dk.at[:, own_columns],
                     out_send.at[3], out_recv.at[3], to_b, z)
                send(dv_s.at[part, :], dv.at[:, own_columns],
                     out_send.at[4], out_recv.at[4], to_b, z)

        @pl.when(helper)
        def _():
            slot = pl.ds(pl.multiple_of((b // 2) * rows, rows), rows)
            for to_b in range(nb):
                part = pl.ds(to_b * rows, rows)
                send(dk_s.at[part, :], dk_part.at[slot, :],
                     out_send.at[3], part_recv.at[0], to_b, z)
                send(dv_s.at[part, :], dv_part.at[slot, :],
                     out_send.at[4], part_recv.at[1], to_b, z)

    wide_columns = pl.ds(pl.multiple_of(z * group, group), group)
    for at, (mid, out) in enumerate(((po_mid, po), (to_mid, to))):
        arrived(mid, mid_recv.at[at])
        swap_planes(lambda plane: mid.at[pl.ds(plane * few, few), :],
                    out.at[:, wide_columns], at, mid_send, out_recv)
    sums = ((dk_part, dk_sum, dk), (dv_part, dv_sum, dv))
    for at, (part, result, out) in enumerate(sums):
        arrived(part, part_recv.at[at])
        held = part[pl.ds(0, rows), :].astype(jnp.float32)
        for step in range(1, nb // 2):
            held += part[pl.ds(step * rows, rows), :].astype(jnp.float32)
        result[...] = held.astype(jnp.bfloat16)
        pltpu.make_async_copy(result, out.at[:, pl.ds(last * HD, HD)], sum_sem.at[at]).start()

    for at, (part, result, out) in enumerate(sums):
        pltpu.make_async_copy(result, out.at[:, pl.ds(last * HD, HD)], sum_sem.at[at]).wait()
    for at, ref in enumerate((po, to, dq)):
        arrived(ref, out_recv.at[at])
    for at, ref in enumerate((dk, dv)):
        arrived(ref.at[:, pl.ds(0, last * HD)], out_recv.at[at + 3])

    for at in range(2):
        arrived(po_mid.at[pl.ds(0, (nh - 1) * few), :], mid_send.at[at])
    arrived(g_in.at[:, pl.ds(0, (nh - 1) * group)], mid_send.at[2])

    def tiles_left(count, sem):
        arrived(kk.at[pl.ds(0, count * rows), pl.ds(0, HD)], sem)

    for role, in_keys, in_queries in (
        (owner, last - 1 + nb // 2, last),
        (helper, last + nb // 2 - 1, last),
        (idle, last + nb // 2, hc),
    ):
        @pl.when(role)
        def _():
            for src, dst, half, at in keys:
                tiles_left(in_keys, in_send.at[at])
            for src, dst, half, at in queries:
                tiles_left(in_queries, in_send.at[at])
            if role is owner:
                for at in range(5):
                    tiles_left(nb - 1, out_send.at[at])
            if role is helper:
                for at in range(3):
                    tiles_left(1, out_send.at[at])
                for at in range(3, 5):
                    tiles_left(nb - 1, out_send.at[at])


def hand_over(*refs):
    sources, outs, held, sem = refs[:5], refs[5:10], refs[10:15], refs[15]
    loads = [pltpu.make_async_copy(sources[at], held[at], sem.at[0, at]) for at in range(5)]
    stores = [pltpu.make_async_copy(held[at], outs[at], sem.at[1, at]) for at in range(5)]
    for copy in loads:
        copy.start()
    for load, store in zip(loads, stores):
        load.wait()
        store.start()
    for copy in stores:
        copy.wait()


def per_device(nb, nh, q, k, v, tq, tk, tv, g):
    rows, feat = q.shape
    hc = feat // HD
    seq = rows * nb
    low = jnp.bfloat16
    anywhere = pl.BlockSpec(memory_space=pl.ANY)
    wide = jax.ShapeDtypeStruct(g.shape, low)
    narrow = jax.ShapeDtypeStruct(q.shape, low)
    shapes = (wide, wide, narrow, narrow, narrow)
    results = pl.pallas_call(
        functools.partial(kernel, nb, nh, hc),
        out_shape=shapes,
        in_specs=[anywhere] * 7,
        out_specs=(anywhere,) * 5,
        scratch_shapes=[
            pltpu.VMEM((seq, 2 * HD), low),
            pltpu.VMEM((seq, 2 * HD), low),
            pltpu.VMEM((seq, 2 * HD), low),
            pltpu.VMEM((seq, HD), low),
            pltpu.VMEM((2 * HD, seq), low),
            pltpu.VMEM((HD, seq), low),
            pltpu.VMEM((seq, HD), low),
            pltpu.VMEM((seq, HD), low),
            pltpu.VMEM((seq, HD), low),
            pltpu.VMEM((seq, HD), low),
            pltpu.VMEM((seq, HD), low),
            pltpu.VMEM((seq, HD), jnp.float32),
            pltpu.VMEM((seq, HD), jnp.float32),
            pltpu.VMEM((rows, feat), low),
            pltpu.VMEM((rows, feat), low),
            pltpu.VMEM((rows, feat), low),
            pltpu.VMEM((nb // 2 * rows, HD), low),
            pltpu.VMEM((nb // 2 * rows, HD), low),
            pltpu.VMEM((rows, HD), low),
            pltpu.VMEM((rows, HD), low),
            pltpu.SemaphoreType.DMA((7,)),
            pltpu.SemaphoreType.DMA((7,)),
            pltpu.SemaphoreType.DMA((5,)),
            pltpu.SemaphoreType.DMA((5,)),
            pltpu.SemaphoreType.DMA((3,)),
            pltpu.SemaphoreType.DMA((3,)),
            pltpu.SemaphoreType.DMA((2,)),
            pltpu.SemaphoreType.DMA((2,)),
        ],
        compiler_params=pltpu.CompilerParams(
            collective_id=0, has_side_effects=True, vmem_limit_bytes=58 * 2**20
        ),
    )(q, k, v, tq, tk, tv, g)
    return pl.pallas_call(
        hand_over,
        out_shape=shapes,
        in_specs=[anywhere] * 5,
        out_specs=(anywhere,) * 5,
        scratch_shapes=[pltpu.VMEM(shape.shape, low) for shape in shapes]
        + [pltpu.SemaphoreType.DMA((2, 5))],
    )(*results)


def solution(mesh):
    nb, nh = mesh.shape["blk"], mesh.shape["head"]
    narrow = P("blk", "head")
    wide = P(("blk", "head"), None)
    return jax.shard_map(
        functools.partial(per_device, nb, nh),
        mesh=mesh,
        in_specs=(narrow,) * 6 + (wide,),
        out_specs=(wide, wide, narrow, narrow, narrow),
        check_vma=False,
    )
```

time: 58.6 us -> 44.3 us (0.76)
  the two profiles are of different devices: /device:TPU:0 before, /device:TPU:7 now
where the time goes in v2:
time: 44.3 us; the launch traced here: 44.1 us
  Pallas kernels  43.5 us (98%)
  between operations  0.64 us (1%)
    pallas_call x1, Pallas kernels, per_device(): pl.pallas_call(functools.partial(kernel, nb, nh, hc), out_shape=shapes, i...  41.5 us
    pallas_call x1, Pallas kernels, per_device(): pl.pallas_call(hand_over, out_shape=shapes, in_specs=[anywhere] * 5, out_...  1.99 us

profile of v2, /device:TPU:7, one launch (start us, length us, event | category | flops | bytes accessed | tf_op | source)
XLA Modules:
  0.0 44.1 jit_solution(14713935959951194338)
XLA Ops:
  0.6 41.5 %shard_map.110 = (bf16[32,2560]{1,0:T(8,128)(2,1)}, bf16[32,2560]{1,0:T(8,128)(2,1)}, bf16[128,640]{1,0:T(8,128)(2,1)}, bf16[128,640]{1,0:T(8,128)(2,1)}, bf16[128,640]{1,0:T(8,128)(2,1)}) custom-call(bf16[128,640]{1,0:T(8,128)(2,1)} %q_in.1, bf16[128,640]{1,0:T(8,128)(2,1)} %k_in.1, bf16[128,640]{1,0:T(8,128)(2,1)} %v_in.1, bf16[128,640]{1,0:T(8,128)(2,1)} %tq_in.1, ...), custom_call_target="tpu_custom_call" | custom-call | tf_op jit(solution)/shard_map/pallas_call | solution.py:264
  42.1 2.0 %shard_map.111 = (bf16[32,2560]{1,0:T(8,128)(2,1)}, bf16[32,2560]{1,0:T(8,128)(2,1)}, bf16[128,640]{1,0:T(8,128)(2,1)}, bf16[128,640]{1,0:T(8,128)(2,1)}, bf16[128,640]{1,0:T(8,128)(2,1)}) custom-call(bf16[32,2560]{1,0:T(8,128)(2,1)} %get-tuple-element.10.refs_0_, bf16[32,2560]{1,0:T(8,128)(2,1)} %get-tuple-element.11.refs_1_, ...), custom_call_target="tpu_custom_call" | custom-call | tf_op jit(solution)/shard_map/pallas_call | solution.py:303

commit v3 on v2

--- a/solution.py
+++ b/solution.py
@@ -72,12 +72,13 @@
         pltpu.make_async_copy(ref, ref, sem).wait()
 
     def swap_planes(src_of, dst, at, s_sems, r_sems):
-        for plane in range(nh):
+        for step in range(nh):
+            plane = (z + 1 + step) % nh
             send(src_of(plane), dst, s_sems.at[at], r_sems.at[at], b, plane)
 
     my_rows = pl.ds(pl.multiple_of(b * rows, rows), rows)
     few_rows = pl.ds(pl.multiple_of(z * few, few), few)
-    swap_planes(lambda plane: g_in.at[:, pl.ds(plane * group, group)],
+    swap_planes(lambda plane: g_in.at[:, pl.ds(pl.multiple_of(plane * group, HD), group)],
                 g_mid.at[few_rows, :], 2, mid_send, mid_recv)
 
     keys = ((k_in, kk, 0, 0), (tk_in, kk, 1, 2), (v_in, vv, 0, 4), (tv_in, vv, 1, 5))
@@ -89,12 +90,14 @@
             arrived(g_mid, mid_recv.at[2])
         tail = src.at[:, pl.ds(last * HD, HD)]
         place = dst.at[my_rows, pl.ds(half * HD, HD)]
-        for head in range(last):
-            send(src.at[:, pl.ds(head * HD, HD)], place,
+        for step in range(last):
+            head = step
+            send(src.at[:, pl.ds(pl.multiple_of(head * HD, HD), HD)], place,
                  in_send.at[at], in_recv.at[at], 2 * head, z)
         if at in (0, 2, 4, 5):
             for step in range(nb // 2):
-                send(tail, place, in_send.at[at], in_recv.at[at], 2 * step + 1, z)
+                to_b = 2 * step + 1
+                send(tail, place, in_send.at[at], in_recv.at[at], to_b, z)
         else:
             send(tail, place, in_send.at[at], in_recv.at[at], 2 * (b // 2) + 1, z)
 
@@ -102,9 +105,12 @@
 
     @pl.when(jnp.logical_not(idle))
     def _():
-        for src, dst, half, at in keys:
+        for src, dst, half, at in keys[:2]:
             arrived(dst.at[:, pl.ds(half * HD, HD)], in_recv.at[at])
-        for src, dst, half, at in queries:
+
+        def await_queries(member):
+            src, dst, half, at = member
+
             @pl.when(owner)
             def _():
                 arrived(dst.at[:, pl.ds(half * HD, HD)], in_recv.at[at])
@@ -116,12 +122,14 @@
                            pl.ds(half * HD, HD)],
                     in_recv.at[at],
                 )
-        vt[...] = vv[...].T
+        await_queries(queries[0])
+        await_queries(queries[1])
         kt[...] = kk[:, :HD].T
         dk_acc[...] = jnp.zeros_like(dk_acc)
         dv_acc[...] = jnp.zeros_like(dv_acc)
 
-        def one_block(i, carry):
+        def one_block(turn, carry):
+            i = (b // 2 + 1 - odd + turn) % (nb // 2)
             at = pl.ds(pl.multiple_of(i * block, block), block)
             pair = qq[at, :]
             query = pair[:, HD:]
@@ -134,6 +142,14 @@
             tan_total = jnp.sum(wt, axis=0, keepdims=True)
             w_low = w.astype(jnp.bfloat16)
             t_low = wt.astype(jnp.bfloat16)
+
+            @pl.when(turn == 0)
+            def _():
+                for src, dst, half, at in keys[2:]:
+                    arrived(dst.at[:, pl.ds(half * HD, HD)], in_recv.at[at])
+                await_queries(queries[2])
+                vt[...] = vv[...].T
+
             sums = nn_dot(vt[...], w_low)
             more = nn_dot(vt[:HD, :], t_low)
             r = 1.0 / total
@@ -165,16 +181,16 @@
                      out_send.at[2], out_recv.at[2], to_b, z)
             return carry
 
-        first = odd * (b // 2)
         count = odd + (1 - odd) * (seq // block)
-        lax.fori_loop(first, first + count, one_block, 0)
+        lax.fori_loop(0, count, one_block, 0)
         dk_s[...] = (dk_acc[...] * inverse).astype(jnp.bfloat16)
         dv_s[...] = dv_acc[...].astype(jnp.bfloat16)
 
         @pl.when(owner)
         def _():
-            for to_b in range(nb):
-                part = pl.ds(to_b * rows, rows)
+            for step in range(nb):
+                to_b = step
+                part = pl.ds(pl.multiple_of(to_b * rows, rows), rows)
                 send(dk_s.at[part, :], dk.at[:, own_columns],
                      out_send.at[3], out_recv.at[3], to_b, z)
                 send(dv_s.at[part, :], dv.at[:, own_columns],
@@ -183,8 +199,9 @@
         @pl.when(helper)
         def _():
             slot = pl.ds(pl.multiple_of((b // 2) * rows, rows), rows)
-            for to_b in range(nb):
-                part = pl.ds(to_b * rows, rows)
+            for step in range(nb):
+                to_b = step
+                part = pl.ds(pl.multiple_of(to_b * rows, rows), rows)
                 send(dk_s.at[part, :], dk_part.at[slot, :],
                      out_send.at[3], part_recv.at[0], to_b, z)
                 send(dv_s.at[part, :], dv_part.at[slot, :],
@@ -193,7 +210,7 @@
     wide_columns = pl.ds(pl.multiple_of(z * group, group), group)
     for at, (mid, out) in enumerate(((po_mid, po), (to_mid, to))):
         arrived(mid, mid_recv.at[at])
-        swap_planes(lambda plane: mid.at[pl.ds(plane * few, few), :],
+        swap_planes(lambda plane: mid.at[pl.ds(pl.multiple_of(plane * few, few), few), :],
                     out.at[:, wide_columns], at, mid_send, out_recv)
     sums = ((dk_part, dk_sum, dk), (dv_part, dv_sum, dv))
     for at, (part, result, out) in enumerate(sums):

time: 44.3 us -> 43.5 us (0.982)
  the two profiles are of different devices: /device:TPU:7 before, /device:TPU:0 now
where the time goes in v3:
time: 43.5 us; the launch traced here: 43.3 us
  Pallas kernels  42.7 us (98%)
  between operations  0.64 us (1%)
    pallas_call x1, Pallas kernels, per_device(): pl.pallas_call(functools.partial(kernel, nb, nh, hc), out_shape=shapes, i...  40.7 us
    pallas_call x1, Pallas kernels, per_device(): pl.pallas_call(hand_over, out_shape=shapes, in_specs=[anywhere] * 5, out_...  1.99 us

profile of v3, /device:TPU:0, one launch (start us, length us, event | category | flops | bytes accessed | tf_op | source)
XLA Modules:
  0.0 43.3 jit_solution(12522592141308897000)
XLA Ops:
  0.6 40.7 %shard_map.110 = (bf16[32,2560]{1,0:T(8,128)(2,1)}, bf16[32,2560]{1,0:T(8,128)(2,1)}, bf16[128,640]{1,0:T(8,128)(2,1)}, bf16[128,640]{1,0:T(8,128)(2,1)}, bf16[128,640]{1,0:T(8,128)(2,1)}) custom-call(bf16[128,640]{1,0:T(8,128)(2,1)} %q_in.1, bf16[128,640]{1,0:T(8,128)(2,1)} %k_in.1, bf16[128,640]{1,0:T(8,128)(2,1)} %v_in.1, bf16[128,640]{1,0:T(8,128)(2,1)} %tq_in.1, ...), custom_call_target="tpu_custom_call" | custom-call | tf_op jit(solution)/shard_map/pallas_call | solution.py:281
  41.3 2.0 %shard_map.111 = (bf16[32,2560]{1,0:T(8,128)(2,1)}, bf16[32,2560]{1,0:T(8,128)(2,1)}, bf16[128,640]{1,0:T(8,128)(2,1)}, bf16[128,640]{1,0:T(8,128)(2,1)}, bf16[128,640]{1,0:T(8,128)(2,1)}) custom-call(bf16[32,2560]{1,0:T(8,128)(2,1)} %get-tuple-element.10.refs_0_, bf16[32,2560]{1,0:T(8,128)(2,1)} %get-tuple-element.11.refs_1_, ...), custom_call_target="tpu_custom_call" | custom-call | tf_op jit(solution)/shard_map/pallas_call | solution.py:320
